TPU v7x, 256 devices: a whole 4x4x8 slice. The times are simulated.
256 devices in a mesh: seg: 8 (over y, x_lo), dp: 32 (over x_hi, z, core).
Axes of the slice: x: 4 (x_hi: 2, x_lo: 2; x = x_hi * 2 + x_lo), y: 4, z: 8, core: 2. Of those that a mesh axis runs over, the one named last changes fastest.
Arguments:
- segment_x: bfloat16 [32, 8, 256, 8192], P('dp', 'seg'), may hold values from -6 to 6
- header_x: bfloat16 [32, 256, 8192], P('dp', 'seg'), may hold values from -6 to 6
- queries: bfloat16 [32, 8, 256, 4096], P('dp', 'seg'), may hold values from -100 to 100
- keys: bfloat16 [32, 8, 256, 512], P('dp', 'seg'), may hold values from -6 to 6
- mem_queries: bfloat16 [32, 8, 128, 512], P('dp', 'seg'), may hold values from -100 to 100
- mem_keys: bfloat16 [32, 8, 128, 512], P('dp', 'seg'), may hold values from -6 to 6
- header_keys: bfloat16 [32, 256, 512], P('dp', 'seg'), may hold values from -6 to 6
- memory_init: float32 [32, 128, 512], P('dp'), may hold values from -6 to 6
- block_mask: int32 [32, 8, 2, 5], P('dp', 'seg'), may hold values from 0 to 1, as said below
- grad_out: bfloat16 [32, 8, 256, 4096], P('dp', 'seg'), may hold values from -6 to 6
- value_weight: bfloat16 [8192, 512], P('dp'), may hold values from -0.0625 to 0.0625
Outputs:
- attention: bfloat16 [32, 8, 256, 4096], P('dp', 'seg')
- value_grad: float32 [8192, 512], P('dp')
Inputs may be any that keep to these rules, and one draw needn't show every extreme that they name: `block_mask`: the entry of a query block for the segment block on its diagonal is 1; entries for later segment blocks are 0.
All inputs are finite; a program needn't handle non-finite values.
Results may differ from a plain program's by a relative error of at most 0.0056.
Values may be sent and summed in bfloat16 or wider, within the bound.
A program may use at most 128 MiB of HBM per device.

v0:
```python
import jax
import jax.numpy as jnp
from jax import lax
from jax.sharding import PartitionSpec as P

HD = 128
BLK = 128


def carried_in(array, axis, combine, identity, reverse):
    count, position = (lax.axis_size(axis), lax.axis_index(axis))
    everything = lax.all_gather(array, axis)
    start = jnp.broadcast_to(jnp.asarray(identity, array.dtype), array.shape)

    def hop(k, before):
        at = count - 1 - k if reverse else k
        reached = at > position if reverse else at < position
        new = combine(before, everything[at])
        return jnp.where(reached, new, before)

    return lax.fori_loop(0, count, hop, start)


def masked_softmax(scores, allowed):
    kept_scores = jnp.where(allowed, scores, -1e30)
    largest = jnp.max(kept_scores, axis=-1, keepdims=True)
    weights = jnp.exp(kept_scores - largest) * allowed.astype(scores.dtype)
    return weights / jnp.sum(weights, axis=-1, keepdims=True)


def allowed_table(block_rows, seg_len, header_len, mem_len):
    header_blocks = header_len // BLK
    per_row = jnp.repeat(block_rows, BLK, axis=0)
    per_key = jnp.concatenate(
        [
            jnp.repeat(per_row[:, :header_blocks], BLK, axis=1),
            jnp.repeat(per_row[:, header_blocks : header_blocks + 1], mem_len, axis=1),
            jnp.repeat(per_row[:, header_blocks + 1 :], BLK, axis=1),
        ],
        axis=1,
    )
    position = jnp.arange(seg_len)
    causal = jnp.concatenate(
        [
            jnp.ones((seg_len, header_len + mem_len), jnp.bool_),
            position[None, :] <= position[:, None],
        ],
        axis=1,
    )
    return (per_key > 0) & causal


def add_sum(earlier, later):
    return earlier + later


def per_device(
    segment_x,
    header_x,
    queries,
    keys,
    mem_queries,
    mem_keys,
    header_keys,
    memory_init,
    block_mask,
    grad_out,
    value_weight,
):
    seq_x = segment_x[0, 0]
    head_x = header_x[0]
    seg_len, width = seq_x.shape
    kv_width = value_weight.shape[1]
    kv_heads = kv_width // HD
    groups = queries.shape[3] // kv_width
    mem_rows = mem_keys.shape[2]
    scale_factor = HD ** (-0.5)
    highest = lax.Precision.HIGHEST
    piece = lax.all_gather(value_weight, "dp", axis=0, tiled=True)
    seg_cols = seq_x
    head_cols = head_x
    seg_sums = jnp.dot(seg_cols, piece, preferred_element_type=jnp.float32)
    head_sums = jnp.dot(head_cols, piece, preferred_element_type=jnp.float32)
    values = seg_sums.astype(jnp.bfloat16)
    head_vals = head_sums.astype(jnp.bfloat16)
    all_head_keys, all_head_vals = (
        lax.all_gather(header_keys[0], "seg", axis=0, tiled=True),
        lax.all_gather(head_vals, "seg", axis=0, tiled=True),
    )
    header_len = all_head_keys.shape[0]
    seg_keys = keys[0, 0].reshape(seg_len, kv_heads, HD)
    value_heads = values.reshape(seg_len, kv_heads, HD)
    read_scores = (
        jnp.einsum(
            "mgd,jgd->gmj",
            mem_queries[0, 0].reshape(mem_rows, kv_heads, HD),
            seg_keys,
            preferred_element_type=jnp.float32,
        )
        * scale_factor
    )
    read_weights = jax.nn.softmax(read_scores, axis=-1).astype(jnp.bfloat16)
    readout = jnp.einsum(
        "gmj,jgd->mgd", read_weights, value_heads, preferred_element_type=jnp.float32
    )
    earlier = carried_in(readout, "seg", add_sum, jnp.zeros_like(readout), False)
    mem_values = (memory_init[0].reshape(mem_rows, kv_heads, HD) + earlier).astype(jnp.bfloat16)
    all_keys = jnp.concatenate(
        [
            all_head_keys.reshape(header_len, kv_heads, HD),
            mem_keys[0, 0].reshape(mem_rows, kv_heads, HD),
            seg_keys,
        ],
        axis=0,
    )
    all_values = jnp.concatenate(
        [all_head_vals.reshape(header_len, kv_heads, HD), mem_values, value_heads], axis=0
    )
    allowed = allowed_table(block_mask[0, 0], seg_len, header_len, mem_rows)
    scores = (
        jnp.einsum(
            "igtd,jgd->gtij",
            queries[0, 0].reshape(seg_len, kv_heads, groups, HD),
            all_keys,
            preferred_element_type=jnp.float32,
        )
        * scale_factor
    )
    weights = masked_softmax(scores, allowed[None, None]).astype(jnp.bfloat16)
    output = (
        jnp.einsum("gtij,jgd->igtd", weights, all_values, preferred_element_type=jnp.float32)
        .reshape(seg_len, kv_width * groups)
        .astype(jnp.bfloat16)
    )
    key_grads = jnp.einsum(
        "gtij,igtd->jgd",
        weights,
        grad_out[0, 0].reshape(seg_len, kv_heads, groups, HD),
        preferred_element_type=jnp.float32,
    )
    mem_grad = key_grads[header_len : header_len + mem_rows]
    later = carried_in(mem_grad, "seg", add_sum, jnp.zeros_like(mem_grad), True)
    read_back = jnp.einsum(
        "gmj,mgd->jgd",
        read_weights.astype(jnp.float32),
        later,
        precision=highest,
        preferred_element_type=jnp.float32,
    )
    value_grads = (
        (key_grads[header_len + mem_rows :] + read_back)
        .reshape(seg_len, kv_width)
        .astype(jnp.bfloat16)
    )
    head_grad = lax.psum_scatter(
        key_grads[:header_len].reshape(header_len, kv_width), "seg", scatter_dimension=0, tiled=True
    )
    contract = (((0,), (0,)), ((), ()))
    seg_cols = seq_x
    head_cols = head_x.astype(jnp.float32)
    owned = lax.psum_scatter(
        lax.dot_general(seg_cols, value_grads, contract, preferred_element_type=jnp.float32)
        + lax.dot_general(
            head_cols, head_grad, contract, precision=highest, preferred_element_type=jnp.float32
        ),
        "dp",
        scatter_dimension=0,
        tiled=True,
    )
    weight_grad = lax.psum(owned, "seg")
    return (output[None, None], weight_grad)


def solution(mesh):
    placed = (
        P("dp", "seg", None, None),
        P("dp", "seg", None),
        P("dp", "seg", None, None),
        P("dp", "seg", None, None),
        P("dp", "seg", None, None),
        P("dp", "seg", None, None),
        P("dp", "seg", None),
        P("dp", None, None),
        P("dp", "seg", None, None),
        P("dp", "seg", None, None),
        P("dp", None),
    )
    return jax.shard_map(
        per_device,
        mesh=mesh,
        in_specs=placed,
        out_specs=(P("dp", "seg", None, None), P("dp", None)),
        check_vma=False,
    )
```

profile of v0, /device:TPU:2, one launch (start us, length us, event | category | flops | bytes accessed | tf_op | source)
XLA Modules:
  0.0 666.7 jit_solution(16481427173922830646)
XLA Ops:
  8.2 1.1 copy.53
  9.5 3.4 copy.89
  12.9 29.2 %all-gather.1 = bf16[1,256,512]{2,1,0:T(8,128)(2,1)S(1)} all-gather(bf16[1,32,512]{2,1,0:T(8,128)(2,1)S(1)} %copy-done.5), channel_id=3, replica_groups=mesh['seg'=8,'dp'=32] {'seg'}, dimensions={1}, use_global_device_ids=true | all-gather | bytes 294912 | tf_op jit(solution)/shard_map/all_gather | solution.py:87
  44.0 3.3 copy.83
  47.3 1.0 fusion.52
  48.4 13.4 %fusion.55 = (f32[4,8,256]{2,1,0:T(8,128)S(1)}, f32[4,8,256,640]{2,3,1,0:T(8,128)}) fusion(f32[256,640]{0,1:T(8,128)} %get-tuple-element.269, pred[256,640]{0,1:T(8,128)(4,1)} %get-tuple-element.270, bf16[256,4,8,128]{3,2,1,0:T(8,128)(2,1)} %bitcast.114, bf16[256,4,128]{2,0,1:T(8,128)(2,1)S(1)} %copy.66, bf16[128,4,128]{2,0,1:T(8,128)(2,1)} %copy.65, ...), kind=kOutput, calls=%fused_computation.57 | convolution fusion | flops 1370358400 | bytes 24576000 | tf_op jit(solution)/shard_map/sub | solution.py:27
  61.8 12.9 %divide_convert_fusion = bf16[4,8,256,640]{2,3,1,0:T(8,128)(2,1)} fusion(f32[4,8,256,640]{2,3,1,0:T(8,128)} %get-tuple-element.274, f32[4,8,256]{2,1,0:T(8,128)S(1)} %get-tuple-element.273), kind=kLoop, calls=%fused_computation.5 | loop fusion | flops 10485760 | bytes 31490048 | tf_op jit(solution)/shard_map/convert_element_type | solution.py:129
  74.7 7.3 %convolution_bitcast_fusion = f32[640,4,128]{0,2,1:T(8,128)S(1)} fusion(bf16[4,8,256,640]{2,3,1,0:T(8,128)(2,1)} %divide_convert_fusion, bf16[256,4,8,128]{0,3,2,1:T(8,128)(2,1)S(1)} %bitcast.107), kind=kOutput, calls=%fused_computation.20 | convolution fusion | flops 1342177280 | bytes 13893632 | tf_op jit(solution)/shard_map/gtij,igtd->jgd/dot_general | solution.py:135
  82.0 1.0 copy-done.1
  83.1 1.0 copy.85
  84.2 1.7 slice.31
  86.9 1.1 fusion.60
  88.0 36.2 %reduce-scatter.7.cloned.1.call-done = f32[32,512]{1,0:T(8,128)} async-done(((f32[256,512]{1,0:T(8,128)}), f32[32,512]{1,0:T(8,128)}) %reduce-scatter.7.cloned.1.call-update) | async-done | bytes 65552
  124.2 11.0 %fusion.30 = f32[512,8192]{1,0:T(8,128)} fusion(f32[32,512]{1,0:T(8,128)} %reduce-scatter.7.cloned.1.call-done, bf16[1,32,8192]{2,1,0:T(8,128)(2,1)S(1)} %copy-done), kind=kOutput, calls=%fused_computation.38 | convolution fusion | flops 1610612736 | bytes 17367040 | tf_op jit(solution)/shard_map/dot_general | solution.py:163
  135.2 45.8 %all-gather.11.cloned.1.call-done = f32[1024,4,128]{0,2,1:T(8,128)} async-done(((f32[128,4,128]{0,2,1:T(8,128)}), f32[1024,4,128]{0,2,1:T(8,128)}) %all-gather.11.cloned.1.call-update) | async-done | bytes 2097168 | tf_op jit(solution)/shard_map/all_gather | solution.py:12
  181.0 2.0 copy.84
  183.0 102.8 %all-gather.7.cloned.1.call-done = bf16[8192,512]{1,0:T(8,128)(2,1)} async-done(((bf16[256,512]{1,0:T(8,128)(2,1)}), bf16[8192,512]{1,0:T(8,128)(2,1)}) %all-gather.7.cloned.1.call-update) | async-done | bytes 8388624 | tf_op jit(solution)/shard_map/all_gather | solution.py:79
  285.8 7.7 %fusion.22 = bf16[256,512]{1,0:T(8,128)(2,1)} fusion(bf16[8192,512]{1,0:T(8,128)(2,1)} %all-gather.7.cloned.1.call-done, bf16[1,1,256,8192]{3,2,1,0:T(8,128)(2,1)} %param.15), kind=kOutput, calls=%fused_computation.27 | convolution fusion | flops 2147614720 | bytes 12845056 | tf_op jit(solution)/shard_map/dot_general | solution.py:82
  293.5 1.1 copy.87
  294.6 1.8 convolution_bitcast_fusion.2
  296.4 2.9 while.31
  299.4 1.7 fusion.21
  301.1 15.3 %add_bitcast_fusion = f32[8192,512]{0,1:T(8,128)} fusion(f32[512,8192]{1,0:T(8,128)} %fusion.30, bf16[256,512]{0,1:T(8,128)(2,1)S(1)} %bitcast.124, bf16[1,1,256,8192]{3,2,1,0:T(8,128)(2,1)} %param.15), kind=kOutput, calls=%fused_computation.7 | convolution fusion | flops 2151677952 | bytes 38010880 | tf_op jit(solution)/shard_map/dot_general | solution.py:162
  318.2 5.0 convolution_convert_fusion.1
  323.2 30.3 %all_gather.22 = bf16[256,512]{1,0:T(8,128)(2,1)S(1)} all-gather(bf16[32,512]{1,0:T(8,128)(2,1)S(1)} %convolution_convert_fusion.1), channel_id=1, replica_groups=mesh['seg'=8,'dp'=32] {'seg'}, dimensions={0}, use_global_device_ids=true | all-gather | bytes 294912 | tf_op jit(solution)/shard_map/all_gather | solution.py:88
  353.7 2.0 copy.82
  355.7 2.9 while.30
  359.7 217.8 %reduce-scatter.5.cloned.1.call-done = f32[256,512]{0,1:T(8,128)} async-done(((f32[8192,512]{0,1:T(8,128)}), f32[256,512]{0,1:T(8,128)}) %reduce-scatter.5.cloned.1.call-update) | async-done | bytes 524304 | tf_op jit(solution)/shard_map/reduce_scatter | solution.py:161
  577.6 5.8 convolution_convert_fusion
  583.4 2.9 copy.73
  586.2 71.6 %all-reduce.3.cloned.1.call-done = f32[256,512]{0,1:T(8,128)} async-done(((f32[256,512]{0,1:T(8,128)}), f32[256,512]{0,1:T(8,128)}) %all-reduce.3.cloned.1.call-update) | async-done | bytes 524304 | tf_op jit(solution)/shard_map/psum | solution.py:170
  657.8 2.0 copy.74
  (62 shorter events, 12.8 us)
Async XLA Ops:
  7.2 117.0 %copy-start = (bf16[1,32,8192]{2,1,0:T(8,128)(2,1)S(1)}, bf16[1,32,8192]{2,1,0:T(8,128)(2,1)}, u32[]{:S(2)}) copy-start(bf16[1,32,8192]{2,1,0:T(8,128)(2,1)} %param.16) | copy-start | bytes 1572868
  7.2 5.7 copy-start.5
  7.2 35.9 %copy-start.3 = (bf16[1,1,128,512]{3,2,1,0:T(8,128)(2,1)S(1)}, bf16[1,1,128,512]{3,2,1,0:T(8,128)(2,1)}, u32[]{:S(2)}) copy-start(bf16[1,1,128,512]{3,2,1,0:T(8,128)(2,1)} %param.20) | copy-start | bytes 393220
  7.2 117.0 %reduce-scatter.7.cloned.1.call-start = ((), (), s32[]{:S(2)}) async-start(), calls=%async_computation.7 | async-start | bytes 589824
  74.7 12.2 %copy-start.4 = (bf16[1,1,128,512]{3,2,1,0:T(8,128)(2,1)S(1)}, bf16[1,1,128,512]{3,2,1,0:T(8,128)(2,1)}, u32[]{:S(2)}) copy-start(bf16[1,1,128,512]{3,2,1,0:T(8,128)(2,1)} %param.19) | copy-start | bytes 393220
  82.0 1.1 copy-start.1
  84.1 96.8 %all-gather.11.cloned.1.call-start = ((), (), s32[]{:S(2)}) async-start(), calls=%async_computation.6 | async-start | bytes 2359296 | tf_op jit(solution)/shard_map/all_gather | solution.py:12
  85.9 200.0 %all-gather.7.cloned.1.call-start = ((), (), s32[]{:S(2)}) async-start(), calls=%async_computation.2 | async-start | bytes 8650752 | tf_op jit(solution)/shard_map/all_gather | solution.py:79
  86.6 267.0 %all-gather.9.cloned.1.call-start = ((), (), s32[]{:S(2)}) async-start(), calls=%async_computation.5 | async-start | bytes 2359296 | tf_op jit(solution)/shard_map/all_gather | solution.py:12
  296.4 281.1 %reduce-scatter.5.cloned.1.call-start = ((), (), s32[]{:S(2)}) async-start(), calls=%async_computation.3 | async-start | bytes 17301504 | tf_op jit(solution)/shard_map/reduce_scatter | solution.py:161
  316.4 0.9 copy-start.2
  316.4 341.4 %all-reduce.3.cloned.1.call-start = ((), (), s32[]{:S(2)}) async-start(), calls=%async_computation.4 | async-start | bytes 1048576 | tf_op jit(solution)/shard_map/psum | solution.py:170
Sparse Core Ops, SparseCore 0:
  84.2 39.9 reduce-scatter.6
  126.0 54.8 all-gather.10
  184.1 101.6 all-gather.6
  296.5 55.3 all-gather.8
  357.1 220.4 reduce-scatter.4
  580.0 77.7 all-reduce.2
where the time goes:
time: 669 us; the launch traced here: 667 us
  waiting for transfers between devices  475 us (71%)
  matrix products  70.1 us (10%)
  blocking collectives  59.5 us (9%)
  local copies, waits for them, and re-layouts  26.6 us (4%)
  other arithmetic  20.5 us (3%)
  between operations  14.3 us (2%)
    reduce_scatter x1, waiting for transfers between devices, per_device(): lax.psum_scatter(lax.dot_general(seg_cols, value_grads, contract, preferr...  218 us
    all_gather x1, waiting for transfers between devices, per_device(): piece = lax.all_gather(value_weight, 'dp', axis=0, tiled=True)  103 us
    psum x1, waiting for transfers between devices, per_device(): weight_grad = lax.psum(owned, 'seg')  71.6 us
    all_gather x2, waiting for transfers between devices, carried_in(): everything = lax.all_gather(array, axis)  45.8 us
    unnamed x7, waiting for transfers between devices  37 us
    all_gather x1, blocking collectives, per_device(): lax.all_gather(head_vals, 'seg', axis=0, tiled=True)  30.3 us
    all_gather x1, blocking collectives, per_device(): lax.all_gather(header_keys[0], 'seg', axis=0, tiled=True)  29.2 us
    unnamed x23, local copies, waits for them, and re-layouts  17.4 us
  transfers between devices with their start and end apart: 6, of which 5 were waited for; matrix products, arithmetic and copies ran while one was open for 8% of the time, Pallas kernels for 0%

commit v1 on v0

v1 whole, which is shorter than its diff:
```python
import functools

import jax
import jax.numpy as jnp
from jax import lax
from jax.experimental import pallas as pl
from jax.experimental.pallas import tpu as pltpu
from jax.sharding import PartitionSpec as P

MESH = pl.DeviceIdType.MESH
BF = jnp.bfloat16
F32 = jnp.float32
NEG = -1e30
HD = 128
SEG = 256
MEM = 128
HDR = 256
G = 4
T = 8
NK = HDR + MEM + SEG
LOG2E = 1.4426950408889634
SCALE2 = HD ** (-0.5) * LOG2E


def device(x, y, z, c):
    return {"seg": y * 2 + x % 2, "dp": (x // 2) * 16 + z * 2 + c}


def kernel(
    seg_x,
    hdr_x,
    q_hbm,
    keys,
    memq,
    memk,
    hkeys,
    minit,
    mask,
    go_hbm,
    w_hbm,
    out_hbm,
    dw_ref,
    q_v,
    go_v,
    out_v,
    wts,
    kall,
    hk_all,
    bias,
    rw,
    kgt,
    xall,
    wb1,
    wb2,
    mg_send,
    mg_recv,
    hs_send,
    hs_recv,
    hg,
    hg_sib,
    vgt,
    vgcat,
    r1,
    r2,
    ra1,
    ra2,
    s1,
    s2,
    rb1,
    rb2,
    t1,
    t2,
    zr1,
    zr2,
    fall,
    acc,
    vrecv,
    v_all,
    hv_all,
    ro_send,
    ro_recv,
    vcat,
    load_sem,
    x_sem,
    seg_s,
    seg_r,
    mg_s,
    mg_r,
    hs_s,
    hs_r,
    sib_s,
    sib_r,
    z_s,
    z_r,
    ring_s,
    ring_r,
):
    s = lax.axis_index("seg")
    p = lax.axis_index("dp")
    y, xl = s // 2, s % 2
    xh, z, c = p // 16, (p // 2) % 8, p % 2
    x = xh * 2 + xl
    k_own = xh * 8 + z
    sib = {"seg": s, "dp": xh * 16 + z * 2 + (1 - c)}
    seg_peer = [{"seg": (s + j) % 8, "dp": p} for j in range(1, 8)]
    z_peer = [device(x, y, (z + j) % 8, c) for j in range(1, 8)]
    rings = {
        "x": (x, device((x + 1) % 4, y, z, c), device((x + 3) % 4, y, z, c)),
        "y": (y, device(x, (y + 1) % 4, z, c), device(x, (y + 3) % 4, z, c)),
    }
    sends = []

    def remote(src, dst, ssem, rsem, dev):
        return pltpu.make_async_remote_copy(
            src_ref=src,
            dst_ref=dst,
            send_sem=ssem,
            recv_sem=rsem,
            device_id=dev,
            device_id_type=MESH,
        )

    def go_out(src, dst, ssem, rsem, dev):
        copy = remote(src, dst, ssem, rsem, dev)
        copy.start()
        sends.append((None, copy))
        return copy

    loads = []
    for g in range(G):
        cols = pl.ds(g * 1024, 1024)
        a = pltpu.make_async_copy(q_hbm.at[0, 0, :, cols], q_v.at[:, cols], load_sem.at[2 * g])
        b = pltpu.make_async_copy(go_hbm.at[0, 0, :, cols], go_v.at[:, cols], load_sem.at[2 * g + 1])
        a.start()
        b.start()
        loads.append((a, b))

    @pl.loop(0, 16)
    def _(k):
        cols = pl.ds(pl.multiple_of((2 * k + c) * 256, 256), 256)
        pltpu.make_async_copy(
            seg_x.at[0, 0, :, cols], xall.at[k, pl.ds(0, 256)], load_sem.at[8]
        ).start()
        pltpu.make_async_copy(
            hdr_x.at[0, :, cols], xall.at[k, pl.ds(512, 32)], load_sem.at[9]
        ).start()

    w_row = s * 32
    own_w = [
        pltpu.make_async_copy(
            w_hbm.at[pl.ds(pl.multiple_of(w_row + 16 * h, 16), 16)], dst, load_sem.at[10 + h]
        )
        for h, dst in ((0, wb1.at[y, x, z]), (1, wb2.at[x, y, z]))
    ]
    for copy in own_w:
        copy.start()

    barrier = pltpu.get_barrier_semaphore()
    greeted = [sib, rings["x"][1], rings["x"][2]] + seg_peer + z_peer
    for dev in greeted:
        pl.semaphore_signal(barrier, inc=1, device_id=dev, device_id_type=MESH)
    pl.semaphore_wait(barrier, len(greeted))

    hk_copies = [
        go_out(hkeys.at[0], hk_all.at[s], seg_s.at[0, j], seg_r.at[0, j], seg_peer[j])
        for j in range(7)
    ]
    wz_copies = []
    for j in range(7):
        for h, dst in ((0, wb1.at[y, x, z]), (1, wb2.at[x, y, z])):
            src = w_hbm.at[pl.ds(pl.multiple_of(w_row + 16 * h, 16), 16)]
            wz_copies.append(go_out(src, dst, z_s.at[h, j], z_r.at[h, j], z_peer[j]))

    @pl.loop(0, 16)
    def _(k):
        cols = pl.ds(pl.multiple_of((2 * k + 1 - c) * 256, 256), 256)
        remote(
            seg_x.at[0, 0, :, cols], xall.at[k, pl.ds(256, 256)], x_sem.at[0], x_sem.at[1], sib
        ).start()
        remote(
            hdr_x.at[0, :, cols], xall.at[k, pl.ds(544, 32)], x_sem.at[2], x_sem.at[3], sib
        ).start()

    hk_all[s] = hkeys[0]
    for k in range(16):
        xall[k, 576:640] = jnp.zeros((64, 256), BF)

    rows_i = lax.broadcasted_iota(jnp.int32, (128, 128), 0)
    cols_i = lax.broadcasted_iota(jnp.int32, (128, 128), 1)
    causal = jnp.where(cols_i <= rows_i, 0.0, NEG).astype(F32)
    for qb in range(2):
        for kb in range(5):
            level = jnp.where(mask[0, 0, qb, kb] > 0, 0.0, NEG).astype(F32)
            block = jnp.full((128, 128), level, F32)
            if kb == 3 + qb:
                block = jnp.minimum(block, causal)
            bias[qb * 128 : qb * 128 + 128, kb * 128 : kb * 128 + 128] = block

    def softmax2(scores):
        top = jnp.max(scores, axis=-1, keepdims=True)
        e = jnp.exp2(scores - top)
        return e * (1.0 / jnp.sum(e, axis=-1, keepdims=True))

    nt = (((1,), (1,)), ((), ()))
    tn = (((0,), (0,)), ((), ()))
    for g in range(G):
        cg = slice(g * 128, g * 128 + 128)
        kall[g, 256:384] = memk[0, 0, :, cg]
        kall[g, 384:640] = keys[0, 0, :, cg]
        sc = lax.dot_general(memq[0, 0, :, cg], keys[0, 0, :, cg], nt, preferred_element_type=F32)
        rw[g] = softmax2(sc * SCALE2).astype(BF)

    for copy in hk_copies:
        copy.wait_recv()
    for g in range(G):
        for t in range(8):
            kall[g, t * 32 : t * 32 + 32] = hk_all[t, :, g * 128 : g * 128 + 128]

    def ag_start(buf, axis, n, st):
        r, right, left = rings[axis]
        lo, hi = pl.ds(0, n // 2), pl.ds(n // 2, n // 2)
        S, R = ring_s.at[st], ring_r.at[st]
        cp = {}
        cp["Llo"] = go_out(buf.at[r, lo], buf.at[r, lo], S.at[0], R.at[0], right)
        cp["Rhi"] = go_out(buf.at[r, hi], buf.at[r, hi], S.at[3], R.at[3], left)
        cp["Lhi"] = go_out(buf.at[r, hi], buf.at[r, hi], S.at[1], R.at[1], right)
        cp["Rlo"] = go_out(buf.at[r, lo], buf.at[r, lo], S.at[2], R.at[2], left)
        return cp

    def ag_forward(buf, axis, n, st, cp):
        r, right, left = rings[axis]
        lo, hi = pl.ds(0, n // 2), pl.ds(n // 2, n // 2)
        S, R = ring_s.at[st], ring_r.at[st]
        before, after = (r + 3) % 4, (r + 1) % 4
        cp["Llo"].wait_recv()
        cp["FL"] = go_out(buf.at[before, lo], buf.at[before, lo], S.at[4], R.at[4], right)
        cp["Rhi"].wait_recv()
        cp["FR"] = go_out(buf.at[after, hi], buf.at[after, hi], S.at[5], R.at[5], left)

    def ag_end(cp):
        for name in ("Lhi", "Rlo", "FL", "FR"):
            cp[name].wait_recv()

    def rs_start(buf, land, axis, n, st):
        r, right, left = rings[axis]
        lo, hi = pl.ds(0, n // 2), pl.ds(n // 2, n // 2)
        S, R = ring_s.at[st], ring_r.at[st]
        far, after, before = (r + 2) % 4, (r + 1) % 4, (r + 3) % 4
        cp = {}
        cp["PL"] = go_out(buf.at[far, lo], land.at[0], S.at[0], R.at[0], right)
        cp["PR"] = go_out(buf.at[far, hi], land.at[1], S.at[1], R.at[1], left)
        cp["Lhi"] = go_out(buf.at[after, hi], land.at[3], S.at[3], R.at[3], right)
        cp["Rlo"] = go_out(buf.at[before, lo], land.at[4], S.at[4], R.at[4], left)
        return cp

    def rs_forward(buf, land, axis, n, st, cp):
        r, right, left = rings[axis]
        half = n // 2
        lo, hi = pl.ds(0, half), pl.ds(half, half)
        S, R = ring_s.at[st], ring_r.at[st]
        after, before = (r + 1) % 4, (r + 3) % 4
        cp["PL"].wait_recv()

        @pl.loop(0, half)
        def _(i):
            a = buf[after, i].astype(F32) + land[0, i].astype(F32)
            buf[after, i] = a.astype(BF)

        cp["Llo"] = go_out(buf.at[after, lo], land.at[2], S.at[2], R.at[2], right)
        cp["PR"].wait_recv()

        @pl.loop(0, half)
        def _(i):
            a = buf[before, half + i].astype(F32) + land[1, i].astype(F32)
            buf[before, half + i] = a.astype(BF)

        cp["Rhi"] = go_out(buf.at[before, hi], land.at[5], S.at[5], R.at[5], left)

    def rs_end(buf, land, out, axis, n, cp):
        r = rings[axis][0]
        half = n // 2
        for name in ("Lhi", "Rlo", "Llo", "Rhi"):
            cp[name].wait_recv()
        for part in range(2):

            @pl.loop(0, half)
            def _(i):
                a = buf[r, half * part + i].astype(F32)
                a = a + land[2 + part, i].astype(F32) + land[4 + part, i].astype(F32)
                out[half * part + i] = a.astype(BF)

    mg_copies = {}
    hs_copies = {}

    def attend(g):
        loads[g][0].wait()
        loads[g][1].wait()
        kgt[g] = jnp.zeros((128, NK), F32)

        @pl.loop(0, T)
        def _(t):
            h = g * T + t
            cols = pl.ds(pl.multiple_of(h * 128, 128), 128)
            for qb in range(2):
                nk = 512 + 128 * qb
                rows = slice(qb * 128, qb * 128 + 128)
                sc = lax.dot_general(
                    q_v[rows, cols], kall[g, 0:nk], nt, preferred_element_type=F32
                )
                wt = softmax2(sc * SCALE2 + bias[rows, 0:nk]).astype(BF)
                wts[h, rows, 0:nk] = wt
                if qb == 0:
                    wts[h, rows, 512:640] = jnp.zeros((128, 128), BF)
            kgt[g] += lax.dot_general(go_v[:, cols], wts[h], tn, preferred_element_type=F32)

        mg_send[g] = kgt[g, :, HDR : HDR + MEM].astype(BF)
        for j in range(7):
            copy = remote(
                mg_send.at[g], mg_recv.at[s, g], mg_s.at[g, j], mg_r.at[g, j], seg_peer[j]
            )
            earlier = (s + j + 1) % 8 < s
            pl.when(earlier)(copy.start)
            sends.append((earlier, copy))
            mg_copies[g, j] = copy
        hs_send[g] = kgt[g, :, 0:HDR].T.astype(BF).reshape(8, 32, 128)
        for j in range(7):
            peer = (s + j + 1) % 8
            hs_copies[g, j] = go_out(
                hs_send.at[g, peer], hs_recv.at[g, j], hs_s.at[g, j], hs_r.at[g, j], seg_peer[j]
            )

    sib_copies = []

    def close_group(g):
        rog = acc.at[0:128, 0:128]
        rog[...] = jnp.zeros((128, 128), F32)
        for j in range(7):
            origin = (s + 7 - j) % 8

            @pl.when(origin > s)
            def _():
                mg_copies[g, j].wait_recv()
                rog[...] += mg_recv[origin, g].astype(F32)

        back = jnp.dot(rog[...].astype(BF), rw[g], preferred_element_type=F32)
        vgt[0, g] = (kgt[g, :, HDR + MEM : NK] + back).astype(BF)
        sib_copies.append(go_out(vgt.at[0, g], vgt.at[1, g], sib_s.at[g], sib_r.at[g], sib))
        total = hs_send[g, s].astype(F32)
        for j in range(7):
            hs_copies[g, j].wait_recv()
            total = total + hs_recv[g, j].astype(F32)
        hg[g] = total.astype(BF)
        sib_copies.append(go_out(hg.at[g], hg_sib.at[g], sib_s.at[4 + g], sib_r.at[4 + g], sib))

    attend(0)
    for copy in own_w:
        copy.wait()
    for copy in wz_copies:
        copy.wait_recv()
    wx1 = ag_start(wb1.at[y], "x", 8, 0)
    wy2 = ag_start(wb2.at[x], "y", 8, 1)
    attend(1)
    ag_forward(wb1.at[y], "x", 8, 0, wx1)
    ag_forward(wb2.at[x], "y", 8, 1, wy2)
    close_group(0)
    attend(2)
    ag_end(wx1)
    ag_end(wy2)
    wy1 = ag_start(wb1, "y", 4, 2)
    wx2 = ag_start(wb2, "x", 4, 3)
    close_group(1)
    attend(3)
    close_group(2)
    ag_forward(wb1, "y", 4, 2, wy1)
    ag_forward(wb2, "x", 4, 3, wx2)
    close_group(3)

    pltpu.make_async_copy(
        xall.at[:, pl.ds(0, 256)], xall.at[:, pl.ds(0, 256)], load_sem.at[8]
    ).wait()
    pltpu.make_async_copy(
        xall.at[:, pl.ds(512, 32)], xall.at[:, pl.ds(512, 32)], load_sem.at[9]
    ).wait()
    sib_x = remote(
        xall.at[:, pl.ds(0, 256)], xall.at[:, pl.ds(256, 256)], x_sem.at[0], x_sem.at[1], sib
    )
    sib_hx = remote(
        xall.at[:, pl.ds(512, 32)], xall.at[:, pl.ds(544, 32)], x_sem.at[2], x_sem.at[3], sib
    )
    sib_x.wait_recv()
    sib_hx.wait_recv()
    for copy in sib_copies:
        copy.wait_recv()
    for g in range(G):
        rg = slice(g * 128, g * 128 + 128)
        vgcat[rg, 0:256] = vgt[0, g]
        vgcat[rg, 256:512] = vgt[1, g]
        head = jnp.concatenate(
            [hg[g].astype(F32), hg_sib[g].astype(F32), jnp.zeros((64, 128), F32)], axis=0
        )
        vgcat[rg, 512:640] = head.T.astype(BF)

    @pl.loop(0, 16)
    def _(k):
        kh, kz = k // 8, k % 8
        grad = jnp.dot(vgcat[...], xall[k], preferred_element_type=F32).astype(BF)
        for yy in range(4):
            for xx in range(2):
                i = yy * 2 + xx
                rows = jnp.concatenate(
                    [grad[g * 128 + i * 16 : g * 128 + i * 16 + 16] for g in range(G)], axis=0
                )
                r1[yy, kh * 2 + xx, kz] = rows[:, 0:128]
                r2[kh * 2 + xx, yy, kz] = rows[:, 128:256]

    gy1 = rs_start(r1, ra1, "y", 4, 4)
    gx2 = rs_start(r2, ra2, "x", 4, 5)

    ag_end(wy1)
    ag_end(wx2)
    for q in range(4):
        xs, ws = [], []
        for k in range(4 * q, 4 * q + 4):
            kh, kz = k // 8, k % 8
            xs.append(xall[k, 0:576])
            for yy in range(4):
                for xx in range(2):
                    ws.append(wb1[yy, kh * 2 + xx, kz])
                    ws.append(wb2[kh * 2 + xx, yy, kz])
        part = jnp.dot(
            jnp.concatenate(xs, axis=1), jnp.concatenate(ws, axis=0), preferred_element_type=F32
        )
        if q == 0:
            acc[...] = part
        else:
            acc[...] += part
    va = go_out(
        acc.at[pl.ds(256, 256)], vrecv.at[pl.ds(0, 256)], sib_s.at[8], sib_r.at[8], sib
    )
    vb = go_out(acc.at[pl.ds(544, 32)], vrecv.at[pl.ds(256, 32)], sib_s.at[9], sib_r.at[9], sib)
    va.wait_recv()
    vb.wait_recv()
    hv_all[s] = (acc[512:544] + vrecv[256:288]).astype(BF)
    hv_copies = [
        go_out(hv_all.at[s], hv_all.at[s], seg_s.at[1, j], seg_r.at[1, j], seg_peer[j])
        for j in range(7)
    ]
    v_all[...] = (acc[0:256] + vrecv[0:256]).astype(BF)
    for g in range(G):
        cg = slice(g * 128, g * 128 + 128)
        ro_send[:, cg] = jnp.dot(rw[g], v_all[:, cg], preferred_element_type=F32).astype(BF)
    ro_copies = []
    for j in range(7):
        copy = remote(ro_send, ro_recv.at[s], seg_s.at[2, j], seg_r.at[2, j], seg_peer[j])
        after = (s + j + 1) % 8 > s
        pl.when(after)(copy.start)
        sends.append((after, copy))
        ro_copies.append(copy)

    rs_forward(r1, ra1, "y", 4, 4, gy1)
    rs_forward(r2, ra2, "x", 4, 5, gx2)

    mem = minit[0]
    memory = acc.at[0:128, :]
    for copy in sends:
        if copy[1] is va:
            copy[1].wait_send()
    memory[...] = mem
    for j in range(7):
        origin = (s + 7 - j) % 8

        @pl.when(origin < s)
        def _():
            ro_copies[j].wait_recv()
            memory[...] += ro_recv[origin].astype(F32)

    for copy in hv_copies:
        copy.wait_recv()
    for g in range(G):
        cg = slice(g * 128, g * 128 + 128)
        for t in range(8):
            vcat[g, t * 32 : t * 32 + 32] = hv_all[t, :, cg]
        vcat[g, 256:384] = memory[:, cg].astype(BF)
        vcat[g, 384:640] = v_all[:, cg]

    out_copies = []

    def finish(g):
        @pl.loop(0, T)
        def _(t):
            h = g * T + t
            cols = pl.ds(pl.multiple_of(h * 128, 128), 128)
            out_v[:, cols] = jnp.dot(wts[h], vcat[g], preferred_element_type=F32).astype(BF)

        cols = pl.ds(g * 1024, 1024)
        copy = pltpu.make_async_copy(
            out_v.at[:, cols], out_hbm.at[0, 0, :, cols], load_sem.at[12 + g]
        )
        copy.start()
        out_copies.append(copy)

    finish(0)
    finish(1)
    rs_end(r1, ra1, s1, "y", 4, gy1)
    gx1 = rs_start(s1, rb1, "x", 8, 6)
    rs_end(r2, ra2, s2, "x", 4, gx2)
    gy2 = rs_start(s2, rb2, "y", 8, 7)
    finish(2)
    rs_forward(s1, rb1, "x", 8, 6, gx1)
    rs_forward(s2, rb2, "y", 8, 7, gy2)
    finish(3)
    rs_end(s1, rb1, t1, "x", 8, gx1)
    gz = []
    for j in range(7):
        to = (z + j + 1) % 8
        gz.append(go_out(t1.at[to], zr1.at[j], z_s.at[2, j], z_r.at[2, j], z_peer[j]))
    rs_end(s2, rb2, t2, "y", 8, gy2)
    for j in range(7):
        to = (z + j + 1) % 8
        gz.append(go_out(t2.at[to], zr2.at[j], z_s.at[3, j], z_r.at[3, j], z_peer[j]))
    for copy in gz:
        copy.wait_recv()
    for t_ref, zr, cols in ((t1, zr1, slice(0, 128)), (t2, zr2, slice(128, 256))):
        total = t_ref[z].astype(F32)
        for j in range(7):
            total = total + zr[j].astype(F32)
        fall[s, :, cols] = total
    f_copies = [
        go_out(fall.at[s], fall.at[s], seg_s.at[3, j], seg_r.at[3, j], seg_peer[j])
        for j in range(7)
    ]
    for copy in f_copies:
        copy.wait_recv()
    for g in range(G):
        rows = jnp.concatenate([fall[i, g * 16 : g * 16 + 16] for i in range(8)], axis=0)
        dw_ref[:, g * 128 : g * 128 + 128] = rows.T

    for copy in out_copies:
        copy.wait()
    sib_x.wait_send()
    sib_hx.wait_send()
    for condition, copy in sends:
        if copy is va:
            continue
        if condition is None:
            copy.wait_send()
        else:
            pl.when(condition)(copy.wait_send)


def per_device(*args):
    vmem = pl.BlockSpec(memory_space=pltpu.VMEM)
    hbm = pl.BlockSpec(memory_space=pl.ANY)
    smem = pl.BlockSpec(memory_space=pltpu.SMEM)
    V = pltpu.VMEM
    dma = pltpu.SemaphoreType.DMA
    return pl.pallas_call(
        kernel,
        out_shape=(
            jax.ShapeDtypeStruct((1, 1, SEG, 4096), BF),
            jax.ShapeDtypeStruct((256, 512), F32),
        ),
        in_specs=[hbm, hbm, hbm, vmem, vmem, vmem, vmem, vmem, smem, hbm, hbm],
        out_specs=(hbm, vmem),
        scratch_shapes=[
            V((SEG, 4096), BF),
            V((SEG, 4096), BF),
            V((SEG, 4096), BF),
            V((32, SEG, NK), BF),
            V((G, NK, HD), BF),
            V((8, 32, 512), BF),
            V((SEG, NK), F32),
            V((G, MEM, SEG), BF),
            V((G, HD, NK), F32),
            V((16, 640, 256), BF),
            V((4, 4, 8, 16, 512), BF),
            V((4, 4, 8, 16, 512), BF),
            V((G, HD, MEM), BF),
            V((8, G, HD, MEM), BF),
            V((G, 8, 32, HD), BF),
            V((G, 7, 32, HD), BF),
            V((G, 32, HD), BF),
            V((G, 32, HD), BF),
            V((2, G, HD, SEG), BF),
            V((512, 640), BF),
            V((4, 4, 8, 64, 128), BF),
            V((4, 4, 8, 64, 128), BF),
            V((6, 2, 8, 64, 128), BF),
            V((6, 2, 8, 64, 128), BF),
            V((4, 8, 64, 128), BF),
            V((4, 8, 64, 128), BF),
            V((6, 4, 64, 128), BF),
            V((6, 4, 64, 128), BF),
            V((8, 64, 128), BF),
            V((8, 64, 128), BF),
            V((7, 64, 128), BF),
            V((7, 64, 128), BF),
            V((8, 64, 256), F32),
            V((576, 512), F32),
            V((288, 512), F32),
            V((SEG, 512), BF),
            V((8, 32, 512), BF),
            V((MEM, 512), BF),
            V((8, MEM, 512), BF),
            V((G, NK, HD), BF),
            dma((16,)),
            dma((4,)),
            dma((4, 7)),
            dma((4, 7)),
            dma((G, 7)),
            dma((G, 7)),
            dma((G, 7)),
            dma((G, 7)),
            dma((10,)),
            dma((10,)),
            dma((4, 7)),
            dma((4, 7)),
            dma((8, 6)),
            dma((8, 6)),
        ],
        compiler_params=pltpu.CompilerParams(
            collective_id=0, has_side_effects=True, vmem_limit_bytes=56 * 1024 * 1024
        ),
    )(*args)


def solution(mesh):
    placed = (
        P("dp", "seg", None, None),
        P("dp", "seg", None),
        P("dp", "seg", None, None),
        P("dp", "seg", None, None),
        P("dp", "seg", None, None),
        P("dp", "seg", None, None),
        P("dp", "seg", None),
        P("dp", None, None),
        P("dp", "seg", None, None),
        P("dp", "seg", None, None),
        P("dp", None),
    )
    return jax.shard_map(
        per_device,
        mesh=mesh,
        in_specs=placed,
        out_specs=(P("dp", "seg", None, None), P("dp", None)),
        check_vma=False,
    )
```

time: 669 us -> 126 us (0.19)
  waiting for transfers between devices: 475 us -> 0 us
  Pallas kernels: 0 us -> 121 us
  matrix products: 70.1 us -> 0 us
  blocking collectives: 59.5 us -> 0 us
  local copies, waits for them, and re-layouts: 26.6 us -> 3.98 us
  other arithmetic: 20.5 us -> 0 us
  between operations: 14.3 us -> 0.65 us
    reduce_scatter x1 -> x0, waiting for transfers between devices: 218 us -> none  [per_device(): lax.psum_scatter(lax.dot_general(seg_cols, value_grads, contract, preferr...]
    all_gather x3 -> x0, waiting for transfers between devices: 149 us -> none  [the longest x1 103 us: per_device(): piece = lax.all_gather(value_weight, 'dp', axis=0, tiled=True)]
    pallas_call x0 -> x1, Pallas kernels: none -> 121 us  [per_device(): pl.pallas_call(kernel, out_shape=(jax.ShapeDtypeStruct((1, 1, SEG, 4096),...]
    psum x1 -> x0, waiting for transfers between devices: 71.6 us -> none  [per_device(): weight_grad = lax.psum(owned, 'seg')]
    all_gather x2 -> x0, blocking collectives: 59.5 us -> none  [the longest x1 30.3 us: per_device(): lax.all_gather(head_vals, 'seg', axis=0, tiled=True)]
    dot_general x8 -> x0, matrix products: 55.5 us -> none  [the longest x1 15.3 us: per_device(): lax.dot_general(seg_cols, value_grads, contract, preferred_element_type=j...]
    unnamed x7 -> x0, waiting for transfers between devices: 37 us -> none
    convert_element_type x3 -> x0, other arithmetic: 14.9 us -> none  [the longest x1 12.9 us: per_device(): weights = masked_softmax(scores, allowed[None, None]).astype(jnp.bfloat16)]
  transfers between devices with their start and end apart: 6 -> 0, of which waited for: 5 -> 0; matrix products, arithmetic and copies ran while one was open for 8% -> 0% of each run, Pallas kernels for 0% -> 0%
where the time goes in v1:
time: 126 us
  Pallas kernels  121 us (96%)
  local copies, waits for them, and re-layouts  3.98 us (3%)
    pallas_call x1, Pallas kernels, per_device(): pl.pallas_call(kernel, out_shape=(jax.ShapeDtypeStruct((1, 1, SEG, 4096),...  121 us
    unnamed x4, local copies, waits for them, and re-layouts  3.98 us

profile of v1, /device:TPU:2, one launch (start us, length us, event | category | flops | bytes accessed | tf_op | source)
XLA Modules:
  0.0 126.0 jit_solution(1866535153473162084)
XLA Ops:
  0.6 121.3 %shard_map.122 = (bf16[1,1,256,4096]{3,2,1,0:T(8,128)(2,1)}, f32[256,512]{1,0:T(8,128)}) custom-call(bf16[1,1,256,8192]{3,2,1,0:T(8,128)(2,1)} %seg_x.1, bf16[1,32,8192]{2,1,0:T(8,128)(2,1)} %hdr_x.1, bf16[1,1,256,4096]{3,2,1,0:T(8,128)(2,1)} %q_hbm.1, bf16[1,1,256,512]{3,2,1,0:T(8,128)(2,1)} %keys.1, bf16[1,1,128,512]{3,2,1,0:T(8,128)(2,1)} %memq.1, ...), custom_call_target="tpu_custom_call" | custom-call | tf_op jit(solution)/shard_map/pallas_call | solution.py:557
  122.0 0.0 copy-start
  122.0 3.2 %copy.15 = bf16[1,1,256,4096]{3,2,1,0:T(8,128)(2,1)} copy(bf16[1,1,256,4096]{3,2,1,0:T(8,128)(2,1)} %get-tuple-element.4) | data formatting | bytes 4194304
  125.2 0.0 copy-done
  125.2 0.8 copy.16
Async XLA Ops:
  122.0 3.2 %copy-start = (f32[256,512]{1,0:T(8,128)S(1)}, f32[256,512]{1,0:T(8,128)}, u32[]{:S(2)}) copy-start(f32[256,512]{1,0:T(8,128)} %get-tuple-element.5) | copy-start | bytes 1572868

commit v2 on v1

--- a/solution.py
+++ b/solution.py
@@ -17,6 +17,7 @@
 HDR = 256
 G = 4
 T = 8
+HEADS = 4
 NK = HDR + MEM + SEG
 LOG2E = 1.4426950408889634
 SCALE2 = HD ** (-0.5) * LOG2E
@@ -54,6 +55,9 @@
     wb2,
     mg_send,
     mg_recv,
+    pm_send,
+    pm_recv,
+    rog,
     hs_send,
     hs_recv,
     hg,
@@ -64,6 +68,8 @@
     r2,
     ra1,
     ra2,
+    da1,
+    da2,
     s1,
     s2,
     rb1,
@@ -79,11 +85,16 @@
     hv_all,
     ro_send,
     ro_recv,
+    po_send,
+    po_recv,
+    memory,
     vcat,
     load_sem,
     x_sem,
     seg_s,
     seg_r,
+    f_s,
+    f_r,
     mg_s,
     mg_r,
     hs_s,
@@ -103,6 +114,9 @@
     k_own = xh * 8 + z
     sib = {"seg": s, "dp": xh * 16 + z * 2 + (1 - c)}
     seg_peer = [{"seg": (s + j) % 8, "dp": p} for j in range(1, 8)]
+    pair = {"seg": y * 2 + (1 - xl), "dp": p}
+    below = [{"seg": ((y + 4 - j) % 4) * 2 + xl, "dp": p} for j in (1, 2, 3)]
+    above = [{"seg": ((y + j) % 4) * 2 + xl, "dp": p} for j in (1, 2, 3)]
     z_peer = [device(x, y, (z + j) % 8, c) for j in range(1, 8)]
     rings = {
         "x": (x, device((x + 1) % 4, y, z, c), device((x + 3) % 4, y, z, c)),
@@ -156,7 +170,8 @@
         copy.start()
 
     barrier = pltpu.get_barrier_semaphore()
-    greeted = [sib, rings["x"][1], rings["x"][2]] + seg_peer + z_peer
+    across = [device((x + j) % 4, y, z, c) for j in (1, 2, 3)]
+    greeted = [sib] + across + seg_peer + z_peer
     for dev in greeted:
         pl.semaphore_signal(barrier, inc=1, device_id=dev, device_id_type=MESH)
     pl.semaphore_wait(barrier, len(greeted))
@@ -240,6 +255,32 @@
     def ag_end(cp):
         for name in ("Lhi", "Rlo", "FL", "FR"):
             cp[name].wait_recv()
+
+    around = {
+        "x": (x, [device((x + j) % 4, y, z, c) for j in (1, 2, 3)]),
+        "y": (y, [device(x, (y + j) % 4, z, c) for j in (1, 2, 3)]),
+    }
+
+    def ag_direct(buf, axis, st):
+        r, to = around[axis]
+        S, R = ring_s.at[st], ring_r.at[st]
+        return [go_out(buf.at[r], buf.at[r], S.at[j], R.at[j], to[j]) for j in (1, 0, 2)]
+
+    def rs_direct(buf, land, axis, st):
+        r, to = around[axis]
+        S, R = ring_s.at[st], ring_r.at[st]
+        return [
+            go_out(buf.at[(r + j + 1) % 4], land.at[j], S.at[j], R.at[j], to[j])
+            for j in (1, 0, 2)
+        ]
+
+    def rs_sum(buf, land, out, axis, copies):
+        for copy in copies:
+            copy.wait_recv()
+        total = buf[around[axis][0]].astype(F32)
+        for j in range(3):
+            total = total + land[j].astype(F32)
+        out[...] = total.astype(BF)
 
     def rs_start(buf, land, axis, n, st):
         r, right, left = rings[axis]
@@ -260,20 +301,10 @@
         S, R = ring_s.at[st], ring_r.at[st]
         after, before = (r + 1) % 4, (r + 3) % 4
         cp["PL"].wait_recv()
-
-        @pl.loop(0, half)
-        def _(i):
-            a = buf[after, i].astype(F32) + land[0, i].astype(F32)
-            buf[after, i] = a.astype(BF)
-
+        buf[after, lo] = (buf[after, lo].astype(F32) + land[0].astype(F32)).astype(BF)
         cp["Llo"] = go_out(buf.at[after, lo], land.at[2], S.at[2], R.at[2], right)
         cp["PR"].wait_recv()
-
-        @pl.loop(0, half)
-        def _(i):
-            a = buf[before, half + i].astype(F32) + land[1, i].astype(F32)
-            buf[before, half + i] = a.astype(BF)
-
+        buf[before, hi] = (buf[before, hi].astype(F32) + land[1].astype(F32)).astype(BF)
         cp["Rhi"] = go_out(buf.at[before, hi], land.at[5], S.at[5], R.at[5], left)
 
     def rs_end(buf, land, out, axis, n, cp):
@@ -282,46 +313,54 @@
         for name in ("Lhi", "Rlo", "Llo", "Rhi"):
             cp[name].wait_recv()
         for part in range(2):
-
-            @pl.loop(0, half)
-            def _(i):
-                a = buf[r, half * part + i].astype(F32)
-                a = a + land[2 + part, i].astype(F32) + land[4 + part, i].astype(F32)
-                out[half * part + i] = a.astype(BF)
+            here = pl.ds(half * part, half)
+            a = buf[r, here].astype(F32) + land[2 + part].astype(F32)
+            out[here] = (a + land[4 + part].astype(F32)).astype(BF)
+
+    def guarded(condition, src, dst, ssem, rsem, dev):
+        copy = remote(src, dst, ssem, rsem, dev)
+        pl.when(condition)(copy.start)
+        sends.append((condition, copy))
+        return copy
 
     mg_copies = {}
+    pm_copies = {}
     hs_copies = {}
-
-    def attend(g):
-        loads[g][0].wait()
-        loads[g][1].wait()
-        kgt[g] = jnp.zeros((128, NK), F32)
-
-        @pl.loop(0, T)
+    sib_copies = {}
+
+    def attend(g, part):
+        if part == 0:
+            loads[g][0].wait()
+            loads[g][1].wait()
+            kgt[g] = jnp.zeros((128, NK), F32)
+
+        @pl.loop(0, T // 2 // HEADS)
         def _(t):
-            h = g * T + t
-            cols = pl.ds(pl.multiple_of(h * 128, 128), 128)
-            for qb in range(2):
-                nk = 512 + 128 * qb
-                rows = slice(qb * 128, qb * 128 + 128)
-                sc = lax.dot_general(
-                    q_v[rows, cols], kall[g, 0:nk], nt, preferred_element_type=F32
-                )
-                wt = softmax2(sc * SCALE2 + bias[rows, 0:nk]).astype(BF)
-                wts[h, rows, 0:nk] = wt
-                if qb == 0:
-                    wts[h, rows, 512:640] = jnp.zeros((128, 128), BF)
-            kgt[g] += lax.dot_general(go_v[:, cols], wts[h], tn, preferred_element_type=F32)
-
+            for u in range(HEADS):
+                h = g * T + part * (T // 2) + t * HEADS + u
+                cols = pl.ds(pl.multiple_of(h * 128, 128), 128)
+                for qb in range(2):
+                    nk = 512 + 128 * qb
+                    rows = slice(qb * 128, qb * 128 + 128)
+                    sc = lax.dot_general(
+                        q_v[rows, cols], kall[g, 0:nk], nt, preferred_element_type=F32
+                    )
+                    wt = softmax2(sc * SCALE2 + bias[rows, 0:nk]).astype(BF)
+                    wts[h, rows, 0:nk] = wt
+                    if qb == 0:
+                        wts[h, rows, 512:640] = jnp.zeros((128, 128), BF)
+            for u in range(HEADS):
+                h = g * T + part * (T // 2) + t * HEADS + u
+                cols = pl.ds(pl.multiple_of(h * 128, 128), 128)
+                kgt[g] += lax.dot_general(go_v[:, cols], wts[h], tn, preferred_element_type=F32)
+
+        if part == 0:
+            return
         mg_send[g] = kgt[g, :, HDR : HDR + MEM].astype(BF)
-        for j in range(7):
-            copy = remote(
-                mg_send.at[g], mg_recv.at[s, g], mg_s.at[g, j], mg_r.at[g, j], seg_peer[j]
+        for j in range(3):
+            mg_copies[g, j] = guarded(
+                y > j, mg_send.at[g], mg_recv.at[g, j], mg_s.at[g, j], mg_r.at[g, j], below[j]
             )
-            earlier = (s + j + 1) % 8 < s
-            pl.when(earlier)(copy.start)
-            sends.append((earlier, copy))
-            mg_copies[g, j] = copy
         hs_send[g] = kgt[g, :, 0:HDR].T.astype(BF).reshape(8, 32, 128)
         for j in range(7):
             peer = (s + j + 1) % 8
@@ -329,92 +368,174 @@
                 hs_send.at[g, peer], hs_recv.at[g, j], hs_s.at[g, j], hs_r.at[g, j], seg_peer[j]
             )
 
-    sib_copies = []
-
-    def close_group(g):
-        rog = acc.at[0:128, 0:128]
-        rog[...] = jnp.zeros((128, 128), F32)
-        for j in range(7):
-            origin = (s + 7 - j) % 8
-
-            @pl.when(origin > s)
+    def close_a(g):
+        rog[g] = jnp.zeros((128, 128), F32)
+        for j in range(3):
+
+            @pl.when(y + j + 1 < 4)
             def _():
                 mg_copies[g, j].wait_recv()
-                rog[...] += mg_recv[origin, g].astype(F32)
-
-        back = jnp.dot(rog[...].astype(BF), rw[g], preferred_element_type=F32)
-        vgt[0, g] = (kgt[g, :, HDR + MEM : NK] + back).astype(BF)
-        sib_copies.append(go_out(vgt.at[0, g], vgt.at[1, g], sib_s.at[g], sib_r.at[g], sib))
+                rog[g] += mg_recv[g, j].astype(F32)
+
+        own = jnp.where(xl == 1, kgt[g, :, HDR : HDR + MEM], 0.0)
+        pm_send[g] = (rog[g] + own).astype(BF)
+        pm_copies[g] = go_out(pm_send.at[g], pm_recv.at[g], mg_s.at[g, 3], mg_r.at[g, 3], pair)
         total = hs_send[g, s].astype(F32)
         for j in range(7):
             hs_copies[g, j].wait_recv()
             total = total + hs_recv[g, j].astype(F32)
         hg[g] = total.astype(BF)
-        sib_copies.append(go_out(hg.at[g], hg_sib.at[g], sib_s.at[4 + g], sib_r.at[4 + g], sib))
-
-    attend(0)
-    for copy in own_w:
-        copy.wait()
-    for copy in wz_copies:
-        copy.wait_recv()
-    wx1 = ag_start(wb1.at[y], "x", 8, 0)
-    wy2 = ag_start(wb2.at[x], "y", 8, 1)
-    attend(1)
-    ag_forward(wb1.at[y], "x", 8, 0, wx1)
-    ag_forward(wb2.at[x], "y", 8, 1, wy2)
-    close_group(0)
-    attend(2)
-    ag_end(wx1)
-    ag_end(wy2)
-    wy1 = ag_start(wb1, "y", 4, 2)
-    wx2 = ag_start(wb2, "x", 4, 3)
-    close_group(1)
-    attend(3)
-    close_group(2)
-    ag_forward(wb1, "y", 4, 2, wy1)
-    ag_forward(wb2, "x", 4, 3, wx2)
-    close_group(3)
-
-    pltpu.make_async_copy(
-        xall.at[:, pl.ds(0, 256)], xall.at[:, pl.ds(0, 256)], load_sem.at[8]
-    ).wait()
-    pltpu.make_async_copy(
-        xall.at[:, pl.ds(512, 32)], xall.at[:, pl.ds(512, 32)], load_sem.at[9]
-    ).wait()
+        hcopy = go_out(hg.at[g], hg_sib.at[g], sib_s.at[4 + g], sib_r.at[4 + g], sib)
+        sib_copies[g] = [hcopy]
+
+    def close_b(g):
+        pm_copies[g].wait_recv()
+        later = (rog[g] + pm_recv[g].astype(F32)).astype(BF)
+        back = jnp.dot(later, rw[g], preferred_element_type=F32)
+        vgt[0, g] = (kgt[g, :, HDR + MEM : NK] + back).astype(BF)
+        sib_copies[g].append(
+            go_out(vgt.at[0, g], vgt.at[1, g], sib_s.at[g], sib_r.at[g], sib)
+        )
+
     sib_x = remote(
         xall.at[:, pl.ds(0, 256)], xall.at[:, pl.ds(256, 256)], x_sem.at[0], x_sem.at[1], sib
     )
     sib_hx = remote(
         xall.at[:, pl.ds(512, 32)], xall.at[:, pl.ds(544, 32)], x_sem.at[2], x_sem.at[3], sib
     )
-    sib_x.wait_recv()
-    sib_hx.wait_recv()
-    for copy in sib_copies:
-        copy.wait_recv()
-    for g in range(G):
-        rg = slice(g * 128, g * 128 + 128)
-        vgcat[rg, 0:256] = vgt[0, g]
-        vgcat[rg, 256:512] = vgt[1, g]
+
+    def x_ready():
+        for rows, sem in ((pl.ds(0, 256), load_sem.at[8]), (pl.ds(512, 32), load_sem.at[9])):
+            pltpu.make_async_copy(xall.at[:, rows], xall.at[:, rows], sem).wait()
+        sib_x.wait_recv()
+        sib_hx.wait_recv()
+
+    def weigh(g):
+        for copy in sib_copies[g]:
+            copy.wait_recv()
+        vgcat[:, 0:256] = vgt[0, g]
+        vgcat[:, 256:512] = vgt[1, g]
         head = jnp.concatenate(
             [hg[g].astype(F32), hg_sib[g].astype(F32), jnp.zeros((64, 128), F32)], axis=0
         )
-        vgcat[rg, 512:640] = head.T.astype(BF)
-
-    @pl.loop(0, 16)
-    def _(k):
-        kh, kz = k // 8, k % 8
-        grad = jnp.dot(vgcat[...], xall[k], preferred_element_type=F32).astype(BF)
-        for yy in range(4):
-            for xx in range(2):
-                i = yy * 2 + xx
-                rows = jnp.concatenate(
-                    [grad[g * 128 + i * 16 : g * 128 + i * 16 + 16] for g in range(G)], axis=0
+        vgcat[:, 512:640] = head.T.astype(BF)
+
+        @pl.loop(0, 8)
+        def _(k):
+            for kh in range(2):
+                grad = jnp.dot(vgcat[...], xall[kh * 8 + k], preferred_element_type=F32)
+                grad = grad.astype(BF)
+                for yy in range(4):
+                    for xx in range(2):
+                        i = (yy * 2 + xx) * 16
+                        r1[g, yy, kh * 2 + xx, k] = grad[i : i + 16, 0:128]
+                        r2[g, kh * 2 + xx, yy, k] = grad[i : i + 16, 128:256]
+
+    first = {}
+    second = {}
+    last = {}
+    spread = {}
+
+    def rs_1(g):
+        if g == G - 1:
+            first[g] = (
+                rs_direct(r1.at[g], da1, "y", 4 + 4 * g),
+                rs_direct(r2.at[g], da2, "x", 5 + 4 * g),
+            )
+        else:
+            first[g] = (
+                rs_start(r1.at[g], ra1.at[g], "y", 4, 4 + 4 * g),
+                rs_start(r2.at[g], ra2.at[g], "x", 4, 5 + 4 * g),
+            )
+
+    def rs_2(g):
+        rs_forward(r1.at[g], ra1.at[g], "y", 4, 4 + 4 * g, first[g][0])
+        rs_forward(r2.at[g], ra2.at[g], "x", 4, 5 + 4 * g, first[g][1])
+
+    def rs_3(g):
+        if g == G - 1:
+            rs_sum(r1.at[g], da1, s1.at[g], "y", first[g][0])
+        else:
+            rs_end(r1.at[g], ra1.at[g], s1.at[g], "y", 4, first[g][0])
+        one = rs_direct(s1.at[g], rb1.at[g], "x", 6 + 4 * g)
+        if g == G - 1:
+            rs_sum(r2.at[g], da2, s2.at[g], "x", first[g][1])
+        else:
+            rs_end(r2.at[g], ra2.at[g], s2.at[g], "x", 4, first[g][1])
+        second[g] = (one, rs_direct(s2.at[g], rb2.at[g], "y", 7 + 4 * g))
+
+    def rs_5(g):
+        last[g] = []
+        for part, (s_ref, rb, t_ref, zr, axis) in enumerate(
+            ((s1, rb1, t1, zr1, "x"), (s2, rb2, t2, zr2, "y"))
+        ):
+            rs_sum(s_ref.at[g], rb.at[g], t_ref.at[g], axis, second[g][part])
+            for j in (3, 2, 4, 1, 5, 0, 6):
+                to = (z + j + 1) % 8
+                st = 2 + 2 * g + part
+                last[g].append(
+                    go_out(
+                        t_ref.at[g, to], zr.at[g, j], z_s.at[st, j], z_r.at[st, j], z_peer[j]
+                    )
                 )
-                r1[yy, kh * 2 + xx, kz] = rows[:, 0:128]
-                r2[kh * 2 + xx, yy, kz] = rows[:, 128:256]
-
-    gy1 = rs_start(r1, ra1, "y", 4, 4)
-    gx2 = rs_start(r2, ra2, "x", 4, 5)
+
+    def rs_6(g):
+        for copy in last[g]:
+            copy.wait_recv()
+        for t_ref, zr, cols in ((t1, zr1, slice(0, 128)), (t2, zr2, slice(128, 256))):
+            total = t_ref[g, z].astype(F32)
+            for j in range(7):
+                total = total + zr[g, j].astype(F32)
+            fall[g, s, :, cols] = total
+        spread[g] = [
+            go_out(fall.at[g, s], fall.at[g, s], f_s.at[g, j], f_r.at[g, j], seg_peer[j])
+            for j in range(7)
+        ]
+
+    def rs_7(g):
+        for copy in spread[g]:
+            copy.wait_recv()
+        dw_ref[:, g * 128 : g * 128 + 128] = fall[g].reshape(128, 256).T
+
+    attend(0, 0)
+    attend(0, 1)
+    for copy in own_w:
+        copy.wait()
+    for copy in wz_copies:
+        copy.wait_recv()
+    near = ag_direct(wb1.at[y], "x", 0) + ag_direct(wb2.at[x], "y", 1)
+    attend(1, 0)
+    attend(1, 1)
+    close_a(0)
+    for copy in near:
+        copy.wait_recv()
+    wy1 = ag_start(wb1, "y", 4, 2)
+    wx2 = ag_start(wb2, "x", 4, 3)
+    attend(2, 0)
+    close_b(0)
+    attend(2, 1)
+    close_a(1)
+    x_ready()
+    weigh(0)
+    rs_1(0)
+    attend(3, 0)
+    close_b(1)
+    weigh(1)
+    rs_1(1)
+    attend(3, 1)
+    close_a(2)
+    ag_forward(wb1, "y", 4, 2, wy1)
+    ag_forward(wb2, "x", 4, 3, wx2)
+    rs_2(0)
+    close_b(2)
+    weigh(2)
+    rs_1(2)
+    close_a(3)
+    rs_3(0)
+    rs_2(1)
+    close_b(3)
+    weigh(3)
+    rs_1(3)
 
     ag_end(wy1)
     ag_end(wx2)
@@ -438,6 +559,9 @@
         acc.at[pl.ds(256, 256)], vrecv.at[pl.ds(0, 256)], sib_s.at[8], sib_r.at[8], sib
     )
     vb = go_out(acc.at[pl.ds(544, 32)], vrecv.at[pl.ds(256, 32)], sib_s.at[9], sib_r.at[9], sib)
+    rs_3(1)
+    rs_2(2)
+    rs_5(0)
     va.wait_recv()
     vb.wait_recv()
     hv_all[s] = (acc[512:544] + vrecv[256:288]).astype(BF)
@@ -449,48 +573,51 @@
     for g in range(G):
         cg = slice(g * 128, g * 128 + 128)
         ro_send[:, cg] = jnp.dot(rw[g], v_all[:, cg], preferred_element_type=F32).astype(BF)
-    ro_copies = []
-    for j in range(7):
-        copy = remote(ro_send, ro_recv.at[s], seg_s.at[2, j], seg_r.at[2, j], seg_peer[j])
-        after = (s + j + 1) % 8 > s
-        pl.when(after)(copy.start)
-        sends.append((after, copy))
-        ro_copies.append(copy)
-
-    rs_forward(r1, ra1, "y", 4, 4, gy1)
-    rs_forward(r2, ra2, "x", 4, 5, gx2)
-
-    mem = minit[0]
-    memory = acc.at[0:128, :]
-    for copy in sends:
-        if copy[1] is va:
-            copy[1].wait_send()
-    memory[...] = mem
-    for j in range(7):
-        origin = (s + 7 - j) % 8
-
-        @pl.when(origin < s)
+    ro_copies = [
+        guarded(
+            y + j + 1 < 4, ro_send, ro_recv.at[j], seg_s.at[2, j], seg_r.at[2, j], above[j]
+        )
+        for j in range(3)
+    ]
+    rs_3(2)
+    rs_5(1)
+    rs_6(0)
+
+    memory[...] = jnp.zeros((MEM, 512), F32)
+    for j in range(3):
+
+        @pl.when(y > j)
         def _():
             ro_copies[j].wait_recv()
-            memory[...] += ro_recv[origin].astype(F32)
-
+            memory[...] += ro_recv[j].astype(F32)
+
+    po_send[...] = (memory[...] + jnp.where(xl == 0, ro_send[...].astype(F32), 0.0)).astype(BF)
+    po_copy = go_out(po_send, po_recv, seg_s.at[2, 3], seg_r.at[2, 3], pair)
+    rs_3(3)
+    rs_5(2)
+    rs_6(1)
+    rs_7(0)
     for copy in hv_copies:
         copy.wait_recv()
+    po_copy.wait_recv()
     for g in range(G):
         cg = slice(g * 128, g * 128 + 128)
         for t in range(8):
             vcat[g, t * 32 : t * 32 + 32] = hv_all[t, :, cg]
-        vcat[g, 256:384] = memory[:, cg].astype(BF)
+        total = minit[0, :, cg] + memory[:, cg] + po_recv[:, cg].astype(F32)
+        vcat[g, 256:384] = total.astype(BF)
         vcat[g, 384:640] = v_all[:, cg]
 
     out_copies = []
 
     def finish(g):
-        @pl.loop(0, T)
+        @pl.loop(0, T // 2)
         def _(t):
-            h = g * T + t
-            cols = pl.ds(pl.multiple_of(h * 128, 128), 128)
-            out_v[:, cols] = jnp.dot(wts[h], vcat[g], preferred_element_type=F32).astype(BF)
+            for u in range(2):
+                h = g * T + 2 * t + u
+                cols = pl.ds(pl.multiple_of(h * 128, 128), 128)
+                part = jnp.dot(wts[h], vcat[g], preferred_element_type=F32)
+                out_v[:, cols] = part.astype(BF)
 
         cols = pl.ds(g * 1024, 1024)
         copy = pltpu.make_async_copy(
@@ -500,48 +627,21 @@
         out_copies.append(copy)
 
     finish(0)
+    rs_5(3)
+    rs_6(2)
+    rs_7(1)
     finish(1)
-    rs_end(r1, ra1, s1, "y", 4, gy1)
-    gx1 = rs_start(s1, rb1, "x", 8, 6)
-    rs_end(r2, ra2, s2, "x", 4, gx2)
-    gy2 = rs_start(s2, rb2, "y", 8, 7)
+    rs_6(3)
     finish(2)
-    rs_forward(s1, rb1, "x", 8, 6, gx1)
-    rs_forward(s2, rb2, "y", 8, 7, gy2)
+    rs_7(2)
     finish(3)
-    rs_end(s1, rb1, t1, "x", 8, gx1)
-    gz = []
-    for j in range(7):
-        to = (z + j + 1) % 8
-        gz.append(go_out(t1.at[to], zr1.at[j], z_s.at[2, j], z_r.at[2, j], z_peer[j]))
-    rs_end(s2, rb2, t2, "y", 8, gy2)
-    for j in range(7):
-        to = (z + j + 1) % 8
-        gz.append(go_out(t2.at[to], zr2.at[j], z_s.at[3, j], z_r.at[3, j], z_peer[j]))
-    for copy in gz:
-        copy.wait_recv()
-    for t_ref, zr, cols in ((t1, zr1, slice(0, 128)), (t2, zr2, slice(128, 256))):
-        total = t_ref[z].astype(F32)
-        for j in range(7):
-            total = total + zr[j].astype(F32)
-        fall[s, :, cols] = total
-    f_copies = [
-        go_out(fall.at[s], fall.at[s], seg_s.at[3, j], seg_r.at[3, j], seg_peer[j])
-        for j in range(7)
-    ]
-    for copy in f_copies:
-        copy.wait_recv()
-    for g in range(G):
-        rows = jnp.concatenate([fall[i, g * 16 : g * 16 + 16] for i in range(8)], axis=0)
-        dw_ref[:, g * 128 : g * 128 + 128] = rows.T
+    rs_7(3)
 
     for copy in out_copies:
         copy.wait()
     sib_x.wait_send()
     sib_hx.wait_send()
     for condition, copy in sends:
-        if copy is va:
-            continue
         if condition is None:
             copy.wait_send()
         else:
@@ -576,47 +676,57 @@
             V((4, 4, 8, 16, 512), BF),
             V((4, 4, 8, 16, 512), BF),
             V((G, HD, MEM), BF),
-            V((8, G, HD, MEM), BF),
+            V((G, 3, HD, MEM), BF),
+            V((G, HD, MEM), BF),
+            V((G, HD, MEM), BF),
+            V((G, HD, MEM), F32),
             V((G, 8, 32, HD), BF),
             V((G, 7, 32, HD), BF),
             V((G, 32, HD), BF),
             V((G, 32, HD), BF),
             V((2, G, HD, SEG), BF),
-            V((512, 640), BF),
-            V((4, 4, 8, 64, 128), BF),
-            V((4, 4, 8, 64, 128), BF),
-            V((6, 2, 8, 64, 128), BF),
-            V((6, 2, 8, 64, 128), BF),
-            V((4, 8, 64, 128), BF),
-            V((4, 8, 64, 128), BF),
-            V((6, 4, 64, 128), BF),
-            V((6, 4, 64, 128), BF),
-            V((8, 64, 128), BF),
-            V((8, 64, 128), BF),
-            V((7, 64, 128), BF),
-            V((7, 64, 128), BF),
-            V((8, 64, 256), F32),
+            V((HD, 640), BF),
+            V((G, 4, 4, 8, 16, 128), BF),
+            V((G, 4, 4, 8, 16, 128), BF),
+            V((G - 1, 6, 2, 8, 16, 128), BF),
+            V((G - 1, 6, 2, 8, 16, 128), BF),
+            V((3, 4, 8, 16, 128), BF),
+            V((3, 4, 8, 16, 128), BF),
+            V((G, 4, 8, 16, 128), BF),
+            V((G, 4, 8, 16, 128), BF),
+            V((G, 3, 8, 16, 128), BF),
+            V((G, 3, 8, 16, 128), BF),
+            V((G, 8, 16, 128), BF),
+            V((G, 8, 16, 128), BF),
+            V((G, 7, 16, 128), BF),
+            V((G, 7, 16, 128), BF),
+            V((G, 8, 16, 256), F32),
             V((576, 512), F32),
             V((288, 512), F32),
             V((SEG, 512), BF),
             V((8, 32, 512), BF),
             V((MEM, 512), BF),
-            V((8, MEM, 512), BF),
+            V((3, MEM, 512), BF),
+            V((MEM, 512), BF),
+            V((MEM, 512), BF),
+            V((MEM, 512), F32),
             V((G, NK, HD), BF),
             dma((16,)),
             dma((4,)),
-            dma((4, 7)),
-            dma((4, 7)),
+            dma((3, 7)),
+            dma((3, 7)),
             dma((G, 7)),
             dma((G, 7)),
+            dma((G, 4)),
+            dma((G, 4)),
             dma((G, 7)),
             dma((G, 7)),
             dma((10,)),
             dma((10,)),
-            dma((4, 7)),
-            dma((4, 7)),
-            dma((8, 6)),
-            dma((8, 6)),
+            dma((2 + 2 * G, 7)),
+            dma((2 + 2 * G, 7)),
+            dma((4 + 4 * G, 6)),
+            dma((4 + 4 * G, 6)),
         ],
         compiler_params=pltpu.CompilerParams(
             collective_id=0, has_side_effects=True, vmem_limit_bytes=56 * 1024 * 1024

time: 126 us -> 115 us (0.913)
  Pallas kernels: 121 us -> 110 us
    pallas_call x1, Pallas kernels: 121 us -> 110 us  [per_device(): pl.pallas_call(kernel, out_shape=(jax.ShapeDtypeStruct((1, 1, SEG, 4096),...]
where the time goes in v2:
time: 115 us
  Pallas kernels  110 us (96%)
  local copies, waits for them, and re-layouts  3.98 us (3%)
    pallas_call x1, Pallas kernels, per_device(): pl.pallas_call(kernel, out_shape=(jax.ShapeDtypeStruct((1, 1, SEG, 4096),...  110 us
    unnamed x4, local copies, waits for them, and re-layouts  3.98 us

profile of v2, /device:TPU:2, one launch (start us, length us, event | category | flops | bytes accessed | tf_op | source)
XLA Modules:
  0.0 114.7 jit_solution(2775343132352443317)
XLA Ops:
  0.6 110.1 %shard_map.122 = (bf16[1,1,256,4096]{3,2,1,0:T(8,128)(2,1)}, f32[256,512]{1,0:T(8,128)}) custom-call(bf16[1,1,256,8192]{3,2,1,0:T(8,128)(2,1)} %seg_x.1, bf16[1,32,8192]{2,1,0:T(8,128)(2,1)} %hdr_x.1, bf16[1,1,256,4096]{3,2,1,0:T(8,128)(2,1)} %q_hbm.1, bf16[1,1,256,512]{3,2,1,0:T(8,128)(2,1)} %keys.1, bf16[1,1,128,512]{3,2,1,0:T(8,128)(2,1)} %memq.1, ...), custom_call_target="tpu_custom_call" | custom-call | tf_op jit(solution)/shard_map/pallas_call | solution.py:657
  110.8 0.0 copy-start
  110.8 3.2 %copy.15 = bf16[1,1,256,4096]{3,2,1,0:T(8,128)(2,1)} copy(bf16[1,1,256,4096]{3,2,1,0:T(8,128)(2,1)} %get-tuple-element.4) | data formatting | bytes 4194304
  114.0 0.0 copy-done
  114.0 0.8 copy.16
Async XLA Ops:
  110.8 3.2 %copy-start = (f32[256,512]{1,0:T(8,128)S(1)}, f32[256,512]{1,0:T(8,128)}, u32[]{:S(2)}) copy-start(f32[256,512]{1,0:T(8,128)} %get-tuple-element.5) | copy-start | bytes 1572868

commit v3 on v2

--- a/solution.py
+++ b/solution.py
@@ -31,19 +31,23 @@
     seg_x,
     hdr_x,
     q_hbm,
+    keys_hbm,
+    memq_hbm,
+    memk_hbm,
+    hkeys_hbm,
+    minit_hbm,
+    mask,
+    go_hbm,
+    w_hbm,
+    out_ref,
+    dw_ref,
     keys,
     memq,
     memk,
     hkeys,
     minit,
-    mask,
-    go_hbm,
-    w_hbm,
-    out_hbm,
-    dw_ref,
     q_v,
     go_v,
-    out_v,
     wts,
     kall,
     hk_all,
@@ -51,7 +55,7 @@
     rw,
     kgt,
     xall,
-    wb1,
+    wa,
     wb2,
     mg_send,
     mg_recv,
@@ -140,6 +144,20 @@
         sends.append((None, copy))
         return copy
 
+    small = [
+        pltpu.make_async_copy(src, dst, load_sem.at[12 + i])
+        for i, (src, dst) in enumerate(
+            (
+                (hkeys_hbm, hkeys),
+                (keys_hbm, keys),
+                (memq_hbm, memq),
+                (memk_hbm, memk),
+                (minit_hbm, minit),
+            )
+        )
+    ]
+    for copy in small:
+        copy.start()
     loads = []
     for g in range(G):
         cols = pl.ds(g * 1024, 1024)
@@ -159,12 +177,11 @@
             hdr_x.at[0, :, cols], xall.at[k, pl.ds(512, 32)], load_sem.at[9]
         ).start()
 
-    w_row = s * 32
+    top_rows = w_hbm.at[pl.ds(0, 128)]
+    piece = w_hbm.at[pl.ds(pl.multiple_of(128 + s * 16, 16), 16)]
     own_w = [
-        pltpu.make_async_copy(
-            w_hbm.at[pl.ds(pl.multiple_of(w_row + 16 * h, 16), 16)], dst, load_sem.at[10 + h]
-        )
-        for h, dst in ((0, wb1.at[y, x, z]), (1, wb2.at[x, y, z]))
+        pltpu.make_async_copy(top_rows, wa.at[xh, z], load_sem.at[10]),
+        pltpu.make_async_copy(piece, wb2.at[x, y, z], load_sem.at[11]),
     ]
     for copy in own_w:
         copy.start()
@@ -176,15 +193,23 @@
         pl.semaphore_signal(barrier, inc=1, device_id=dev, device_id_type=MESH)
     pl.semaphore_wait(barrier, len(greeted))
 
+    for copy in small:
+        copy.wait()
+
     hk_copies = [
         go_out(hkeys.at[0], hk_all.at[s], seg_s.at[0, j], seg_r.at[0, j], seg_peer[j])
         for j in range(7)
     ]
-    wz_copies = []
-    for j in range(7):
-        for h, dst in ((0, wb1.at[y, x, z]), (1, wb2.at[x, y, z])):
-            src = w_hbm.at[pl.ds(pl.multiple_of(w_row + 16 * h, 16), 16)]
-            wz_copies.append(go_out(src, dst, z_s.at[h, j], z_r.at[h, j], z_peer[j]))
+    far_first = (3, 2, 4, 1, 5, 0, 6)
+    wz_copies = [
+        go_out(piece, wb2.at[x, y, z], z_s.at[1, j], z_r.at[1, j], z_peer[j]) for j in far_first
+    ]
+    beside = go_out(
+        top_rows, wa.at[xh, z], ring_s.at[0, 0], ring_r.at[0, 0], device(3 - x, y, z, c)
+    )
+    wa_copies = [
+        go_out(top_rows, wa.at[xh, z], z_s.at[0, j], z_r.at[0, j], z_peer[j]) for j in far_first
+    ]
 
     @pl.loop(0, 16)
     def _(k):
@@ -503,13 +528,17 @@
         copy.wait()
     for copy in wz_copies:
         copy.wait_recv()
-    near = ag_direct(wb1.at[y], "x", 0) + ag_direct(wb2.at[x], "y", 1)
+    near = ag_direct(wb2.at[x], "y", 1)
+    beside.wait_recv()
+    other = wa.at[1 - xh, z]
+    st = 2 + 2 * G
+    for j in far_first:
+        wa_copies.append(go_out(other, other, z_s.at[st, j], z_r.at[st, j], z_peer[j]))
     attend(1, 0)
     attend(1, 1)
     close_a(0)
     for copy in near:
         copy.wait_recv()
-    wy1 = ag_start(wb1, "y", 4, 2)
     wx2 = ag_start(wb2, "x", 4, 3)
     attend(2, 0)
     close_b(0)
@@ -524,7 +553,6 @@
     rs_1(1)
     attend(3, 1)
     close_a(2)
-    ag_forward(wb1, "y", 4, 2, wy1)
     ag_forward(wb2, "x", 4, 3, wx2)
     rs_2(0)
     close_b(2)
@@ -537,16 +565,17 @@
     weigh(3)
     rs_1(3)
 
-    ag_end(wy1)
     ag_end(wx2)
+    for copy in wa_copies:
+        copy.wait_recv()
     for q in range(4):
         xs, ws = [], []
         for k in range(4 * q, 4 * q + 4):
             kh, kz = k // 8, k % 8
             xs.append(xall[k, 0:576])
+            ws.append(wa[kh, kz])
             for yy in range(4):
                 for xx in range(2):
-                    ws.append(wb1[yy, kh * 2 + xx, kz])
                     ws.append(wb2[kh * 2 + xx, yy, kz])
         part = jnp.dot(
             jnp.concatenate(xs, axis=1), jnp.concatenate(ws, axis=0), preferred_element_type=F32
@@ -608,8 +637,6 @@
         vcat[g, 256:384] = total.astype(BF)
         vcat[g, 384:640] = v_all[:, cg]
 
-    out_copies = []
-
     def finish(g):
         @pl.loop(0, T // 2)
         def _(t):
@@ -617,14 +644,7 @@
                 h = g * T + 2 * t + u
                 cols = pl.ds(pl.multiple_of(h * 128, 128), 128)
                 part = jnp.dot(wts[h], vcat[g], preferred_element_type=F32)
-                out_v[:, cols] = part.astype(BF)
-
-        cols = pl.ds(g * 1024, 1024)
-        copy = pltpu.make_async_copy(
-            out_v.at[:, cols], out_hbm.at[0, 0, :, cols], load_sem.at[12 + g]
-        )
-        copy.start()
-        out_copies.append(copy)
+                out_ref[0, 0, :, cols] = part.astype(BF)
 
     finish(0)
     rs_5(3)
@@ -637,8 +657,6 @@
     finish(3)
     rs_7(3)
 
-    for copy in out_copies:
-        copy.wait()
     sib_x.wait_send()
     sib_hx.wait_send()
     for condition, copy in sends:
@@ -657,13 +675,17 @@
     return pl.pallas_call(
         kernel,
         out_shape=(
-            jax.ShapeDtypeStruct((1, 1, SEG, 4096), BF),
-            jax.ShapeDtypeStruct((256, 512), F32),
+            pltpu.VMEM((1, 1, SEG, 4096), BF),
+            pltpu.VMEM((256, 512), F32),
         ),
-        in_specs=[hbm, hbm, hbm, vmem, vmem, vmem, vmem, vmem, smem, hbm, hbm],
-        out_specs=(hbm, vmem),
+        in_specs=[hbm] * 8 + [smem, hbm, hbm],
+        out_specs=(vmem, vmem),
         scratch_shapes=[
-            V((SEG, 4096), BF),
+            V((1, 1, SEG, 512), BF),
+            V((1, 1, MEM, 512), BF),
+            V((1, 1, MEM, 512), BF),
+            V((1, 32, 512), BF),
+            V((1, MEM, 512), F32),
             V((SEG, 4096), BF),
             V((SEG, 4096), BF),
             V((32, SEG, NK), BF),
@@ -673,7 +695,7 @@
             V((G, MEM, SEG), BF),
             V((G, HD, NK), F32),
             V((16, 640, 256), BF),
-            V((4, 4, 8, 16, 512), BF),
+            V((2, 8, 128, 512), BF),
             V((4, 4, 8, 16, 512), BF),
             V((G, HD, MEM), BF),
             V((G, 3, HD, MEM), BF),
@@ -711,7 +733,7 @@
             V((MEM, 512), BF),
             V((MEM, 512), F32),
             V((G, NK, HD), BF),
-            dma((16,)),
+            dma((17,)),
             dma((4,)),
             dma((3, 7)),
             dma((3, 7)),
@@ -723,8 +745,8 @@
             dma((G, 7)),
             dma((10,)),
             dma((10,)),
-            dma((2 + 2 * G, 7)),
-            dma((2 + 2 * G, 7)),
+            dma((3 + 2 * G, 7)),
+            dma((3 + 2 * G, 7)),
             dma((4 + 4 * G, 6)),
             dma((4 + 4 * G, 6)),
         ],

time: 115 us -> 110 us (0.957)
  Pallas kernels: 110 us -> 107 us
  local copies, waits for them, and re-layouts: 3.98 us -> 2.11 us
    pallas_call x1, Pallas kernels: 110 us -> 107 us  [per_device(): pl.pallas_call(kernel, out_shape=(pltpu.VMEM((1, 1, SEG, 4096), BF), pltp...]
    unnamed x4 -> x2, local copies, waits for them, and re-layouts: 3.98 us -> 2.11 us
where the time goes in v3:
time: 110 us
  Pallas kernels  107 us (97%)
  local copies, waits for them, and re-layouts  2.11 us (2%)
    pallas_call x1, Pallas kernels, per_device(): pl.pallas_call(kernel, out_shape=(pltpu.VMEM((1, 1, SEG, 4096), BF), pltp...  107 us

profile of v3, /device:TPU:2, one launch (start us, length us, event | category | flops | bytes accessed | tf_op | source)
XLA Modules:
  0.0 109.9 jit_solution(7634217626216347256)
XLA Ops:
  0.6 107.1 %shard_map.122 = (bf16[1,1,256,4096]{3,2,1,0:T(8,128)(2,1)S(1)}, f32[256,512]{1,0:T(8,128)S(1)}) custom-call(bf16[1,1,256,8192]{3,2,1,0:T(8,128)(2,1)} %seg_x.1, bf16[1,32,8192]{2,1,0:T(8,128)(2,1)} %hdr_x.1, bf16[1,1,256,4096]{3,2,1,0:T(8,128)(2,1)} %q_hbm.1, bf16[1,1,256,512]{3,2,1,0:T(8,128)(2,1)} %keys_hbm.1, bf16[1,1,128,512]{3,2,1,0:T(8,128)(2,1)} %memq_hbm.1, ...), custom_call_target="tpu_custom_call" | custom-call | tf_op jit(solution)/shard_map/pallas_call | solution.py:675
  107.8 1.3 %copy.15 = bf16[1,1,256,4096]{3,2,1,0:T(8,128)(2,1)} copy(bf16[1,1,256,4096]{3,2,1,0:T(8,128)(2,1)S(1)} %get-tuple-element.2) | data formatting | bytes 4194304
  109.1 0.8 copy.16
